TPU v7x, 32 devices: a whole 2x2x4 slice. The times are simulated.
32 devices in a mesh: groups: 2 (over x), tp: 8 (over z, y), sub: 2 (over core).
Axes of the slice: x: 2, y: 2, z: 4, core: 2. Of those that a mesh axis runs over, the one named last changes fastest.
Arguments:
- queries: bfloat16 [4096, 12288], P(('groups', 'tp', 'sub')), parts along dimension 0, may hold values from -68 to 68
- new_kv: bfloat16 [4096, 2048], P(('groups', 'tp', 'sub')), parts along dimension 0, may hold values from -6 to 6
- prefix_kv: bfloat16 [4, 4096, 2048], P('groups', 'tp'), parts along dimension 0, may hold values from -6 to 6
- prefix_len: int32 [4], P('groups'), parts along dimension 0, may hold values from 1 to 4096, as said below
- owner: int32 [4096], P(('groups', 'tp', 'sub')), parts along dimension 0, may hold values from 0 to 15, as said below
- slot: int32 [4096], P(('groups', 'tp', 'sub')), parts along dimension 0, may hold values from 0 to 127, as said below
Outputs:
- attended: bfloat16 [4096, 12288], P(('groups', 'tp', 'sub')), parts along dimension 0
- pages: bfloat16 [4096, 2048], P(('groups', 'tp', 'sub')), parts along dimension 0
There are 2 independent parts, one for each index of `groups`. A program takes and returns all parts, laid end to end along the dimension named above; each array names one. Nothing has to cross between parts.
Inputs may be any that keep to these rules, and one draw needn't show every extreme that they name: One prompt in each draw has prefix_len 4096. Among the 128 rows of one device (aligned blocks) at most 9 name the same owner, and in every such block one owner is named by exactly 9 rows; every owner is named by exactly 128 rows in all. The pair (owner, slot) differs from row to row, so every page slot is written once.
All inputs are finite; a program needn't handle non-finite values.
Results may differ from a plain program's by a relative error of at most 0.0049.
Values may be sent and summed in bfloat16 or wider, within the bound.
A program may use at most 128 MiB of HBM per device.

v0:
```python
import jax
import jax.numpy as jnp
import numpy as np
from jax import lax
from jax.sharding import PartitionSpec as P

HEADS = 96
KVH = 8
HS = 128
SPAN = 1024
PMAX = 4096


def softmax_mix(query_head, key_head, value_head, allowed, score_scale):
    scores = jnp.dot(query_head, key_head.T, preferred_element_type=jnp.float32) * score_scale
    scores = jnp.where(allowed, scores, -1e30)
    top_score = jnp.max(scores, axis=1, keepdims=True)
    expo = jnp.where(allowed, jnp.exp(scores - top_score), 0.0)
    total = jnp.sum(expo, axis=1, keepdims=True)
    weights = (expo / total).astype(jnp.bfloat16)
    return jnp.dot(weights, value_head, preferred_element_type=jnp.float32).astype(jnp.bfloat16)


def shards(queries, new_kv, prefix_kv, prefix_len, owner, slot):
    tp_count = lax.axis_size("tp")
    sub_count = lax.axis_size("sub")
    sub_index = lax.axis_index("sub")
    dev_count = tp_count * sub_count
    rows_src = queries.shape[0]
    prompts = prefix_len.shape[0]
    heads_dev = HEADS // tp_count
    group_size = HEADS // KVH
    score_scale = HS ** (-0.5)
    head_of_peer = np.arange(tp_count) * heads_dev // group_size
    kv_local = new_kv.reshape(rows_src, 2, KVH, HS)
    query_send = queries.reshape(rows_src, tp_count, heads_dev * HS)
    query_recv = lax.all_to_all(query_send, "tp", split_axis=1, concat_axis=0, tiled=True)
    dest_heads = np.repeat(head_of_peer, sub_count)
    key_send = jnp.take(kv_local, dest_heads, axis=2)
    key_send = jnp.transpose(key_send, (2, 0, 1, 3)).reshape(dev_count, rows_src, 2 * HS)
    new_keys = lax.all_to_all(
        key_send, ("tp", "sub"), split_axis=0, concat_axis=0, tiled=True
    ).reshape(-1, 2 * HS)
    shard_rows = prefix_kv.shape[1]
    cache_local = prefix_kv.reshape(prompts, shard_rows, 2, KVH, HS)
    prefix_send = jnp.take(cache_local, head_of_peer, axis=3)
    prefix_send = jnp.transpose(prefix_send, (0, 3, 1, 2, 4)).reshape(
        prompts, tp_count, shard_rows, 2 * HS
    )
    cached = lax.all_to_all(prefix_send, "tp", split_axis=1, concat_axis=1, tiled=True)
    cached = cached.reshape(prompts, PMAX, 2, HS)
    local_rows = tp_count * rows_src
    query_rows_all = local_rows // prompts
    arrival = jnp.arange(local_rows)
    global_row = (arrival // rows_src * sub_count + sub_index) * rows_src + arrival % rows_src
    query_pos = (global_row % SPAN).reshape(prompts, query_rows_all)
    query_blocks = query_recv.reshape(prompts, query_rows_all, heads_dev, HS)
    new_blocks = new_keys.reshape(prompts, SPAN, 2, HS)
    column = jnp.arange(PMAX + SPAN)

    def prompt(packed):
        query_rows, positions, new_rows, cache_rows, length = packed
        key_rows = jnp.concatenate([cache_rows[:, 0], new_rows[:, 0]], axis=0)
        value_rows = jnp.concatenate([cache_rows[:, 1], new_rows[:, 1]], axis=0)
        allowed = jnp.where(
            column[None, :] < PMAX,
            column[None, :] < length,
            column[None, :] - PMAX <= positions[:, None],
        )

        def one_head(query_head):
            return softmax_mix(query_head, key_rows, value_rows, allowed, score_scale)

        mixed = lax.map(one_head, jnp.transpose(query_rows, (1, 0, 2)))
        return jnp.transpose(mixed, (1, 0, 2)).reshape(query_rows_all, heads_dev * HS)

    outputs = lax.map(prompt, (query_blocks, query_pos, new_blocks, cached, prefix_len))
    outputs = outputs.reshape(tp_count, rows_src, heads_dev * HS)
    attended = lax.all_to_all(outputs, "tp", split_axis=0, concat_axis=2, tiled=True).reshape(
        rows_src, HEADS * HS
    )
    capacity = max(rows_src // dev_count + 1, 2)
    width = new_kv.shape[1]
    spots = jnp.arange(rows_src)
    same_owner = (owner[:, None] == owner[None, :]) & (spots[None, :] < spots[:, None])
    within = jnp.sum(same_owner.astype(jnp.int32), axis=1)
    flat_index = owner * capacity + within
    send_rows = jnp.zeros((dev_count * capacity, width), jnp.bfloat16).at[flat_index].set(new_kv)
    send_slots = jnp.full((dev_count * capacity,), -1, jnp.int32).at[flat_index].set(slot)
    rows_in, slots_in = (
        lax.all_to_all(
            send_rows.reshape(dev_count, capacity, width),
            ("tp", "sub"),
            split_axis=0,
            concat_axis=0,
            tiled=True,
        ),
        lax.all_to_all(
            send_slots.reshape(dev_count, capacity),
            ("tp", "sub"),
            split_axis=0,
            concat_axis=0,
            tiled=True,
        ),
    )
    slots_flat = slots_in.reshape(-1)
    target = jnp.where(slots_flat >= 0, slots_flat, rows_src)
    pages = (
        jnp.zeros((rows_src, width), jnp.bfloat16)
        .at[target]
        .set(rows_in.reshape(-1, width), mode="drop")
    )
    return (attended, pages)


def solution(mesh):
    placed = (
        P(("groups", "tp", "sub"), None),
        P(("groups", "tp", "sub"), None),
        P("groups", "tp", None),
        P("groups"),
        P(("groups", "tp", "sub")),
        P(("groups", "tp", "sub")),
    )
    return jax.shard_map(
        shards,
        mesh=mesh,
        in_specs=placed,
        out_specs=(P(("groups", "tp", "sub"), None), P(("groups", "tp", "sub"), None)),
        check_vma=False,
    )
```

profile of v0, /device:TPU:0, one launch (start us, length us, event | category | flops | bytes accessed | tf_op | source)
XLA Modules:
  0.0 648.6 jit_solution(15529195799373822590)
XLA Ops:
  5.0 7.4 %all-to-all-start.2 = ((bf16[16,128,256]{1,2,0:T(8,128)(2,1)}), bf16[16,128,256]{1,2,0:T(8,128)(2,1)S(1)}, u32[]{:S(2)}, u32[]{:S(2)}) async-start(bf16[16,128,256]{1,2,0:T(8,128)(2,1)} %bitcast.8), calls=%async_computation.2 | async-start | bytes 2097152 | tf_op jit(solution)/shard_map/all_to_all | solution.py:41
  12.4 4.6 copy.71
  17.0 18.3 %all-to-all-done.2 = bf16[16,128,256]{1,2,0:T(8,128)(2,1)S(1)} async-done(((bf16[16,128,256]{1,2,0:T(8,128)(2,1)}), bf16[16,128,256]{1,2,0:T(8,128)(2,1)S(1)}, u32[]{:S(2)}, u32[]{:S(2)}) %all-to-all-start.2) | async-done | bytes 1048608 | tf_op jit(solution)/shard_map/all_to_all | solution.py:41
  36.4 6.8 %all-to-all-start = ((bf16[128,8,1536]{0,2,1:T(8,128)(2,1)}), bf16[128,8,1536]{0,2,1:T(8,128)(2,1)S(1)}, u32[]{:S(2)}, u32[]{:S(2)}) async-start(bf16[128,8,1536]{0,2,1:T(8,128)(2,1)} %bitcast.86), calls=%async_computation | async-start | bytes 6291456 | tf_op jit(solution)/shard_map/all_to_all | solution.py:37
  43.1 6.3 copy.73
  49.4 6.2 copy.74
  55.6 5.2 gather_fusion
  60.9 4.6 select_bitcast_fusion
  65.5 6.5 %copy.89 = bf16[2,8,512,2,128]{2,4,3,0,1:T(8,128)(2,1)} copy(bf16[2,8,512,2,128]{4,2,3,0,1:T(8,128)(2,1)} %select_bitcast_fusion) | data formatting | bytes 8388608 | tf_op jit(solution)/shard_map/reshape | solution.py:47
  72.0 42.3 %all-to-all-done = bf16[128,8,1536]{0,2,1:T(8,128)(2,1)S(1)} async-done(((bf16[128,8,1536]{0,2,1:T(8,128)(2,1)}), bf16[128,8,1536]{0,2,1:T(8,128)(2,1)S(1)}, u32[]{:S(2)}, u32[]{:S(2)}) %all-to-all-start) | async-done | bytes 3145760 | tf_op jit(solution)/shard_map/all_to_all | solution.py:37
  116.0 4.5 all-to-all-start.1
  122.6 90.8 %all-to-all-done.1 = bf16[2,8,512,256]{2,3,0,1:T(8,128)(2,1)} async-done(((bf16[2,8,512,256]{2,3,0,1:T(8,128)(2,1)}), bf16[2,8,512,256]{2,3,0,1:T(8,128)(2,1)}, u32[]{:S(2)}, u32[]{:S(2)}) %all-to-all-start.1) | async-done | bytes 4194336 | tf_op jit(solution)/shard_map/all_to_all | solution.py:50
  222.4 10.7 %copy.72 = bf16[8,128,1,1536]{1,0,3,2:T(8,128)(2,1)} copy(bf16[8,128,1,1536]{1,3,0,2:T(8,128)(2,1)} %bitcast.85) | data formatting | bytes 6291456 | tf_op jit(solution)/shard_map/all_to_all | solution.py:37
  233.1 5.7 reshape.118
  238.8 8.7 %copy.82 = bf16[2,512,12,128]{3,1,2,0:T(8,128)(2,1)} copy(bf16[2,512,12,128]{1,0,3,2:T(2,128)(2,1)} %reshape.118) | data formatting | bytes 6291456
  247.5 6.5 %copy.77 = bf16[2,8,512,256]{2,1,3,0:T(8,128)(2,1)} copy(bf16[2,8,512,256]{2,3,0,1:T(8,128)(2,1)} %all-to-all-done.1) | data formatting | bytes 8388608 | tf_op jit(solution)/shard_map/all_to_all | solution.py:50
  254.0 7.4 %reshape.121 = bf16[2,4096,2,128]{1,3,2,0:T(8,128)(2,1)} reshape(bf16[2,8,512,256]{2,1,3,0:T(8,128)(2,1)} %copy.77) | data formatting | bytes 8388608 | tf_op jit(solution)/shard_map/reshape | solution.py:51
  261.4 6.1 all-to-all-start.5
  267.5 296.7 %while.37 = (s32[]{:T(128)}, bf16[2,512,1536]{2,1,0:T(8,128)(2,1)}, bf16[2,512,12,128]{3,1,2,0:T(8,128)(2,1)}, bf16[2,4096,2,128]{1,3,2,0:T(8,128)(2,1)}, bf16[2...) while((s32[]{:T(128)}, bf16[2,512,1536]{2,1,0:T(8,128)(2,1)}, ...), condition=%wide.region_5.6_spmd.clone.clone, body=%wide.region_0.5_spmd.clone.clone.sunk | while | flops 1389443072 | bytes 102150744 | solution.py:77
  278.8 134.8 %while.38 = (s32[]{:T(128)}, bf16[12,512,128]{1,2,0:T(8,128)(2,1)S(1)}, bf16[12,512,128]{2,1,0:T(8,128)(2,1)}, bf16[5120,128]{1,0:T(8,128)(2,1)S(1)}, bf16[5120,...) while((s32[]{:T(128)}, ...), condition=%wide.region_4.4_spmd.clone, body=%wide.region_1.3_spmd.clone.sunk | while | flops 1384184832 | bytes 40216720 | solution.py:74
  290.0 3.8 fusion.31
  312.5 3.8 fusion.31
  334.9 3.8 fusion.31
  379.8 3.8 fusion.31
  427.0 134.8 %while.38 = (s32[]{:T(128)}, bf16[12,512,128]{1,2,0:T(8,128)(2,1)S(1)}, bf16[12,512,128]{2,1,0:T(8,128)(2,1)}, bf16[5120,128]{1,0:T(8,128)(2,1)S(1)}, bf16[5120,...) while((s32[]{:T(128)}, ...), condition=%wide.region_4.4_spmd.clone, body=%wide.region_1.3_spmd.clone.sunk | while | flops 1384184832 | bytes 40216720 | solution.py:74
  438.2 3.8 fusion.31
  460.7 3.8 fusion.31
  505.6 3.8 fusion.31
  550.5 3.8 fusion.31
  564.2 6.0 all-to-all-start.3
  576.5 64.6 %all-to-all-done.3 = bf16[8,128,1536]{2,1,0:T(8,128)(2,1)S(1)} async-done(((bf16[8,128,1536]{2,1,0:T(8,128)(2,1)}), bf16[8,128,1536]{2,1,0:T(8,128)(2,1)S(1)}, u32[]{:S(2)}, u32[]{:S(2)}) %all-to-all-start.3) | async-done | bytes 3145760 | tf_op jit(solution)/shard_map/all_to_all | solution.py:79
  644.0 4.6 copy.88
  (258 shorter events, 291.6 us)
Async XLA Ops:
  5.0 30.3 %all-to-all-start.2 = ((bf16[16,128,256]{1,2,0:T(8,128)(2,1)}), bf16[16,128,256]{1,2,0:T(8,128)(2,1)S(1)}, u32[]{:S(2)}, u32[]{:S(2)}) async-start(bf16[16,128,256]{1,2,0:T(8,128)(2,1)} %bitcast.8), calls=%async_computation.2 | async-start | bytes 2097152 | tf_op jit(solution)/shard_map/all_to_all | solution.py:41
  36.4 77.9 %all-to-all-start = ((bf16[128,8,1536]{0,2,1:T(8,128)(2,1)}), bf16[128,8,1536]{0,2,1:T(8,128)(2,1)S(1)}, u32[]{:S(2)}, u32[]{:S(2)}) async-start(bf16[128,8,1536]{0,2,1:T(8,128)(2,1)} %bitcast.86), calls=%async_computation | async-start | bytes 6291456 | tf_op jit(solution)/shard_map/all_to_all | solution.py:37
  114.3 6.3 copy-start.11
  116.0 97.3 %all-to-all-start.1 = ((bf16[2,8,512,256]{2,3,0,1:T(8,128)(2,1)}), bf16[2,8,512,256]{2,3,0,1:T(8,128)(2,1)}, u32[]{:S(2)}, u32[]{:S(2)}) async-start(bf16[2,8,512,256]{2,3,0,1:T(8,128)(2,1)} %bitcast.83), calls=%async_computation.1 | async-start | bytes 8388608 | tf_op jit(solution)/shard_map/all_to_all | solution.py:50
  213.3 48.0 %all-to-all-start.4 = ((s32[16,1,9]{2,1,0:T(1,128)}), s32[16,1,9]{2,1,0:T(1,128)S(1)}, u32[]{:S(2)}, u32[]{:S(2)}) async-start(s32[16,1,9]{2,1,0:T(1,128)} %bitcast.13), calls=%async_computation.4 | async-start | bytes 16384 | tf_op jit(solution)/shard_map/all_to_all | solution.py:98
  254.0 13.5 %copy-start.12 = (s32[2]{0:T(128)S(1)}, s32[2]{0:T(128)}, u32[]{:S(2)}) copy-start(s32[2]{0:T(128)} %param.15) | copy-start | bytes 28
  261.4 6.1 copy-start.9
  261.4 302.8 %all-to-all-start.5 = ((bf16[16,9,2048]{2,1,0:T(8,128)(2,1)}), bf16[16,9,2048]{2,1,0:T(8,128)(2,1)}, u32[]{:S(2)}, u32[]{:S(2)}) async-start(bf16[16,9,2048]{2,1,0:T(8,128)(2,1)} %reshape.127), calls=%async_computation.5 | async-start | bytes 2097152 | tf_op jit(solution)/shard_map/all_to_all | solution.py:91
  267.7 9.7 %copy-start.7 = (s32[2,512]{1,0:T(2,128)}, s32[2,512]{1,0:T(2,128)S(1)}, u32[]{:S(2)}) copy-start(s32[2,512]{1,0:T(2,128)S(1)} %get-tuple-element.483) | copy-start | bytes 12292 | tf_op jit(solution)/shard_map/while
  282.6 3.7 copy-start.2
  293.8 3.7 copy-start.2
  305.1 3.7 copy-start.2
  316.3 3.7 copy-start.2
  327.5 3.7 copy-start.2
  338.7 3.7 copy-start.2
  350.0 3.7 copy-start.2
  361.2 3.7 copy-start.2
  372.4 3.7 copy-start.2
  383.7 3.7 copy-start.2
  394.9 3.7 copy-start.2
  406.1 3.7 copy-start.2
  415.9 9.7 %copy-start.7 = (s32[2,512]{1,0:T(2,128)}, s32[2,512]{1,0:T(2,128)S(1)}, u32[]{:S(2)}) copy-start(s32[2,512]{1,0:T(2,128)S(1)} %get-tuple-element.483) | copy-start | bytes 12292 | tf_op jit(solution)/shard_map/while
  430.8 3.7 copy-start.2
  442.0 3.7 copy-start.2
  453.3 3.7 copy-start.2
  464.5 3.7 copy-start.2
  475.7 3.7 copy-start.2
  487.0 3.7 copy-start.2
  498.2 3.7 copy-start.2
  531.9 3.7 copy-start.2
  564.2 6.6 %copy-start.10 = (s32[16,1,9]{2,1,0:T(1,128)S(1)}, s32[16,1,9]{2,1,0:T(1,128)}, u32[]{:S(2)}) copy-start(s32[16,1,9]{2,1,0:T(1,128)} %copy-done.9) | copy-start | bytes 1732
  564.2 77.0 %all-to-all-start.3 = ((bf16[8,128,1536]{2,1,0:T(8,128)(2,1)}), bf16[8,128,1536]{2,1,0:T(8,128)(2,1)S(1)}, u32[]{:S(2)}, u32[]{:S(2)}) async-start(bf16[8,128,1536]{2,1,0:T(8,128)(2,1)} %bitcast.89), calls=%async_computation.3 | async-start | bytes 6291456 | tf_op jit(solution)/shard_map/all_to_all | solution.py:79
  (18 other events, 48.6 us)
where the time goes:
time: 651 us; the launch traced here: 649 us
  waiting for transfers between devices  216 us (33%)
  matrix products  176 us (27%)
  local copies, waits for them, and re-layouts  121 us (19%)
  other arithmetic  98.8 us (15%)
  starting transfers between devices  34.4 us (5%)
    dot_general x24, matrix products, softmax_mix(): jnp.dot(query_head, key_head.T, preferred_element_type=jnp.float32)  91.9 us
    all_to_all x1, waiting for transfers between devices, shards(): lax.all_to_all(prefix_send, 'tp', split_axis=1, concat_axis=1, tiled=True)  90.8 us
    reduce_sum x24, other arithmetic, softmax_mix(): total = jnp.sum(expo, axis=1, keepdims=True)  88.7 us
    dot_general x24, matrix products, softmax_mix(): jnp.dot(weights, value_head, preferred_element_type=jnp.float32)  84.4 us
    all_to_all x1, waiting for transfers between devices, shards(): lax.all_to_all(outputs, 'tp', split_axis=0, concat_axis=2, tiled=True)  64.6 us
    all_to_all x1, waiting for transfers between devices, shards(): lax.all_to_all(query_send, 'tp', split_axis=1, concat_axis=0, tiled=True)  42.3 us
    unnamed x17, local copies, waits for them, and re-layouts  28.3 us
    all_to_all x1, waiting for transfers between devices, shards(): lax.all_to_all(key_send, ('tp', 'sub'), split_axis=0, concat_axis=0, tile...  18.3 us
  transfers between devices with their start and end apart: 6, of which 4 were waited for; matrix products, arithmetic and copies ran while one was open for 58% of the time, Pallas kernels for 0%

commit v1 on v0

--- a/solution.py
+++ b/solution.py
@@ -2,6 +2,8 @@
 import jax.numpy as jnp
 import numpy as np
 from jax import lax
+from jax.experimental import pallas as pl
+from jax.experimental.pallas import tpu as pltpu
 from jax.sharding import PartitionSpec as P
 
 HEADS = 96
@@ -113,6 +115,303 @@
     return (attended, pages)
 
 
+LOG2E = 1.4426950408889634
+
+
+def attend_kernel(
+    q_ref, new_ref, prefix_ref, bias_ref, o_ref,
+    kv, news, acc, m_s, edge, send_sem, ici_sem, sib_sem, new_sem, newsib_sem, local_sem,
+):
+    t = lax.axis_index("tp")
+    s = lax.axis_index("sub")
+    h = t // 4
+    y = t % 2
+    zl = (t // 2) % 2
+    inner = (h + zl) == 1
+    outer = (h + zl) != 1
+    zp = t + 2 - 4 * zl
+    yp = t + 1 - 2 * y
+    dp = zp + 1 - 2 * y
+    sp = 1 - s
+    near = 4 + y - 2 * h
+    far = 6 * (1 - h) + y
+    near_y = near + 1 - 2 * y
+    far_y = far + 1 - 2 * y
+    rows = new_ref.shape[0]
+    shard = prefix_ref.shape[1]
+    half = shard // 2
+    me = (t % 4) * 2 + s
+
+    def dev(tp, sub):
+        return {"tp": tp, "sub": sub}
+
+    barrier = pltpu.get_barrier_semaphore()
+    for target in (dev(zp, s), dev(yp, s), dev(dp, s), dev(t, sp), dev(near, s)):
+        pl.semaphore_signal(barrier, inc=1, device_id=target, device_id_type=pl.DeviceIdType.MESH)
+
+    @pl.when(inner)
+    def _():
+        pl.semaphore_signal(
+            barrier, inc=1, device_id=dev(far, s), device_id_type=pl.DeviceIdType.MESH
+        )
+        pl.semaphore_wait(barrier, 6)
+
+    @pl.when(outer)
+    def _():
+        pl.semaphore_wait(barrier, 5)
+
+    def copy(src, dst, slot, recv, target):
+        return pltpu.make_async_remote_copy(
+            src_ref=src, dst_ref=dst, send_sem=send_sem.at[slot], recv_sem=recv,
+            device_id=target, device_id_type=pl.DeviceIdType.MESH,
+        )
+
+    def piece(src, part):
+        return kv.at[src, pl.ds(pl.multiple_of(part * half, half), half)]
+
+    def own_piece(prompt):
+        return prefix_ref.at[prompt, pl.ds(pl.multiple_of(s * half, half), half)]
+
+    def new_of(tp, sub):
+        return news.at[(tp % 4) * 2 + sub]
+
+    first = [
+        copy(new_ref, new_of(t, s), 0, new_sem.at[0], dev(zp, s)),
+        copy(new_ref, new_of(t, s), 1, new_sem.at[1], dev(yp, s)),
+        copy(new_ref, new_of(t, s), 2, new_sem.at[2], dev(dp, s)),
+        copy(new_ref, new_of(t, s), 3, newsib_sem.at[3], dev(t, sp)),
+        copy(own_piece(h), piece(t, s), 4, ici_sem.at[0], dev(zp, s)),
+        copy(own_piece(h), piece(t, s), 5, ici_sem.at[3], dev(yp, s)),
+    ]
+    load = pltpu.make_async_copy(prefix_ref.at[h], kv.at[t], local_sem.at[0])
+    load.start()
+    keep = pltpu.make_async_copy(new_ref, news.at[me], local_sem.at[1])
+    keep.start()
+    for one in first:
+        one.start()
+    cross_near = copy(own_piece(1 - h), piece(t, s), 6, ici_sem.at[1], dev(near, s))
+    cross_far = copy(own_piece(1 - h), piece(t, s), 6, ici_sem.at[2], dev(near, s))
+    pl.when(inner)(cross_near.start)
+    pl.when(outer)(cross_far.start)
+
+    def to_sib(role, src):
+        return copy(piece(src, s), piece(src, s), 8 + role, sib_sem.at[role], dev(t, sp))
+
+    def to_y(role, src):
+        return copy(piece(src, s), piece(src, s), 16 + role, ici_sem.at[4 + role], dev(yp, s))
+
+    def to_z(role, src):
+        return copy(piece(src, s), piece(src, s), 20 + role, ici_sem.at[role], dev(zp, s))
+
+    def new_sib(role, tp):
+        return copy(new_of(tp, s), new_of(tp, s), 24 + role, newsib_sem.at[role], dev(t, sp))
+
+    def got(role, src):
+        copy(piece(src, s), piece(src, s), 31, ici_sem.at[role], dev(t, sp)).wait_recv()
+
+    def got_sib(role, src):
+        copy(piece(src, sp), piece(src, sp), 31, sib_sem.at[role], dev(t, sp)).wait_recv()
+
+    def column(role, src):
+        got(role, src)
+        to_y(role, src).start()
+        to_sib(role, src).start()
+
+    def across(role, src):
+        got(role, src)
+        to_sib(role, src).start()
+
+    def column_inner(role, src):
+        got(role, src)
+        to_z(role, src).start()
+        to_y(role, src).start()
+        to_sib(role, src).start()
+
+    scale = HS ** (-0.5) * LOG2E
+    group = HEADS // KVH
+
+    def attend(pieces, bias, start, actions=()):
+        def key_head(g, carry):
+            for step, condition, action in actions:
+                @pl.when((g == step) if condition is None else ((g == step) & condition))
+                def _():
+                    action()
+            key_cols = pl.ds(pl.multiple_of(g * HS, HS), HS)
+            value_cols = pl.ds(pl.multiple_of((KVH + g) * HS, HS), HS)
+            keys = jnp.concatenate([load_cols(key_cols) for load_cols in pieces], axis=0)
+            values = jnp.concatenate([load_cols(value_cols) for load_cols in pieces], axis=0)
+            values = jnp.concatenate([values, jnp.ones_like(values)], axis=1)
+            offset = bias()
+            for i in range(group):
+                at = pl.ds(pl.multiple_of((g * group + i) * HS, HS), HS)
+                at_row = pl.ds(pl.multiple_of((g * group + i) * rows, rows), rows)
+                scores = lax.dot_general(
+                    q_ref[:, at], keys, (((1,), (1,)), ((), ())), preferred_element_type=jnp.float32
+                )
+                scores = scores * scale + offset
+                top = jnp.max(scores, axis=1, keepdims=True)
+                if start:
+                    best = jnp.broadcast_to(top, (rows, HS))
+                else:
+                    old = m_s[at_row, :]
+                    best = jnp.maximum(old, top)
+                weights = jnp.exp2(scores - best[:, :1]).astype(jnp.bfloat16)
+                mixed = jnp.dot(weights, values, preferred_element_type=jnp.float32)
+                if start:
+                    acc[at_row, :] = mixed
+                else:
+                    fade = jnp.exp2(old - best)
+                    acc[at_row, :] = acc[at_row, :] * jnp.concatenate([fade, fade], axis=1) + mixed
+                m_s[at_row, :] = best
+            return carry
+
+        lax.fori_loop(0, KVH, key_head, 0)
+
+    def shard_cols(src):
+        return lambda cols: kv[src, :, cols]
+
+    def shard_bias(src):
+        return bias_ref[:, pl.ds(pl.multiple_of(src * shard, shard), shard)]
+
+    def pair_bias(a, b):
+        return lambda: jnp.concatenate([shard_bias(a), shard_bias(b)], axis=1)
+
+    causal = lax.broadcasted_iota(jnp.int32, (rows, rows), 1) <= lax.broadcasted_iota(
+        jnp.int32, (rows, rows), 0
+    )
+    edge[:, :rows] = jnp.where(causal, 0.0, -1e30)
+    edge[:, rows:] = jnp.broadcast_to(shard_bias(t), (rows, shard))
+    load.wait()
+    attend([lambda cols: new_ref[:, cols], shard_cols(t)], lambda: edge[...], True)
+
+    for role, tp in enumerate((zp, yp, dp)):
+        copy(new_of(tp, s), new_of(tp, s), 31, new_sem.at[role], dev(t, sp)).wait_recv()
+        new_sib(role, tp).start()
+    keep.wait()
+    for role, tp in enumerate((zp, yp, dp, t)):
+        copy(new_of(tp, sp), new_of(tp, sp), 31, newsib_sem.at[role], dev(t, sp)).wait_recv()
+    count = news.shape[0]
+    earlier = lax.broadcasted_iota(jnp.int32, (1, count * rows), 1) < me * rows
+    new_bias = jnp.where(earlier, 0.0, -1e30)
+
+    def arrive_first():
+        column(0, zp)
+        across(3, yp)
+
+    attend(
+        [lambda cols, i=i: news[i, :, cols] for i in range(count)], lambda: new_bias, False,
+        [(7, None, arrive_first), (7, inner, lambda: column_inner(1, near))],
+    )
+    got_sib(0, zp)
+    got_sib(3, yp)
+    attend(
+        [shard_cols(zp), shard_cols(yp)], pair_bias(zp, yp), False,
+        [
+            (4, inner, lambda: column_inner(2, far)),
+            (7, outer, lambda: column(1, near)),
+            (7, None, lambda: across(4, dp)),
+        ],
+    )
+    got_sib(4, dp)
+    got_sib(1, near)
+    attend(
+        [shard_cols(dp), shard_cols(near)], pair_bias(dp, near), False,
+        [
+            (6, outer, lambda: column(2, far)),
+            (7, None, lambda: across(5, near_y)),
+        ],
+    )
+    got_sib(5, near_y)
+    got_sib(2, far)
+    attend(
+        [shard_cols(near_y), shard_cols(far)], pair_bias(near_y, far), False,
+        [(6, None, lambda: across(6, far_y))],
+    )
+    got_sib(6, far_y)
+    attend([shard_cols(far_y)], lambda: shard_bias(far_y), False)
+
+    def finish(i, carry):
+        at = pl.ds(pl.multiple_of(i * HS, HS), HS)
+        at_row = pl.ds(pl.multiple_of(i * rows, rows), rows)
+        o_ref[:, at] = (acc[at_row, :HS] / acc[at_row, HS:]).astype(o_ref.dtype)
+        return carry
+
+    lax.fori_loop(0, HEADS, finish, 0)
+
+    for one in first:
+        one.wait_send()
+    cross_near.wait_send()
+    for role, src in enumerate((zp, near, far, yp, dp, near_y, far_y)):
+        to_sib(role, src).wait_send()
+    for role, src in enumerate((zp, near, far)):
+        to_y(role, src).wait_send()
+    for role, tp in enumerate((zp, yp, dp)):
+        new_sib(role, tp).wait_send()
+
+    @pl.when(inner)
+    def _():
+        to_z(1, near).wait_send()
+        to_z(2, far).wait_send()
+
+
+def send_pages(new_kv, owner, slot):
+    dev_count = lax.axis_size("tp") * lax.axis_size("sub")
+    rows, width = new_kv.shape
+    capacity = max(rows // dev_count + 1, 2)
+    spots = jnp.arange(rows)
+    same_owner = (owner[:, None] == owner[None, :]) & (spots[None, :] < spots[:, None])
+    within = jnp.sum(same_owner.astype(jnp.int32), axis=1)
+    flat_index = owner * capacity + within
+    places = jnp.arange(dev_count * capacity)
+    pick = (places[:, None] == flat_index[None, :]).astype(jnp.bfloat16)
+    marks = jnp.broadcast_to((slot + 1).astype(jnp.bfloat16)[:, None], (rows, HS))
+    packed = jnp.concatenate([new_kv, marks], axis=1)
+    sent = jnp.dot(pick, packed, preferred_element_type=jnp.float32).astype(jnp.bfloat16)
+    rows_in = lax.all_to_all(
+        sent.reshape(dev_count, capacity, width + HS),
+        ("tp", "sub"), split_axis=0, concat_axis=0, tiled=True,
+    ).reshape(dev_count * capacity, width + HS)
+    slots_in = rows_in[:, width].astype(jnp.int32) - 1
+    put = (jnp.arange(rows)[:, None] == slots_in[None, :]).astype(jnp.bfloat16)
+    return jnp.dot(put, rows_in[:, :width], preferred_element_type=jnp.float32).astype(jnp.bfloat16)
+
+
+def fused(queries, new_kv, prefix_kv, prefix_len, owner, slot):
+    rows = queries.shape[0]
+    shard = prefix_kv.shape[1]
+    length = prefix_len[lax.axis_index("tp") // 4]
+    bias = jnp.where(jnp.arange(PMAX)[None, :] < length, 0.0, -1e30).astype(jnp.float32)
+    pages = send_pages(new_kv, owner, slot)
+    vmem = pl.BlockSpec(memory_space=pltpu.VMEM)
+    attended = pl.pallas_call(
+        attend_kernel,
+        out_shape=jax.ShapeDtypeStruct(queries.shape, jnp.bfloat16),
+        in_specs=[vmem, vmem, pl.BlockSpec(memory_space=pl.ANY), vmem],
+        out_specs=vmem,
+        scratch_shapes=[
+            pltpu.VMEM((PMAX // shard, shard, new_kv.shape[1]), jnp.bfloat16),
+            pltpu.VMEM((SPAN // rows, rows, new_kv.shape[1]), jnp.bfloat16),
+            pltpu.VMEM((HEADS * rows, 2 * HS), jnp.float32),
+            pltpu.VMEM((HEADS * rows, HS), jnp.float32),
+            pltpu.VMEM((rows, rows + shard), jnp.float32),
+            pltpu.SemaphoreType.DMA((32,)),
+            pltpu.SemaphoreType.DMA((7,)),
+            pltpu.SemaphoreType.DMA((7,)),
+            pltpu.SemaphoreType.DMA((3,)),
+            pltpu.SemaphoreType.DMA((4,)),
+            pltpu.SemaphoreType.DMA((2,)),
+        ],
+        compiler_params=pltpu.CompilerParams(
+            collective_id=0, has_side_effects=True, vmem_limit_bytes=60 * 2**20
+        ),
+        cost_estimate=pl.CostEstimate(
+            flops=4 * rows * HEADS * HS * (PMAX + SPAN), bytes_accessed=2**23, transcendentals=0
+        ),
+        name="attend",
+    )(queries, new_kv, prefix_kv, bias)
+    return (attended, pages)
+
+
 def solution(mesh):
     placed = (
         P(("groups", "tp", "sub"), None),
@@ -122,8 +421,10 @@
         P(("groups", "tp", "sub")),
         P(("groups", "tp", "sub")),
     )
+    small = mesh.shape["tp"] == 8 and mesh.shape["sub"] == 2
+    body = fused if small else shards
     return jax.shard_map(
-        shards,
+        body,
         mesh=mesh,
         in_specs=placed,
         out_specs=(P(("groups", "tp", "sub"), None), P(("groups", "tp", "sub"), None)),

time: 651 us -> 189 us (0.29)
  waiting for transfers between devices: 216 us -> 0.01 us
  matrix products: 176 us -> 2.45 us
  Pallas kernels: 0 us -> 168 us
  local copies, waits for them, and re-layouts: 121 us -> 6.1 us
  other arithmetic: 98.8 us -> 3.65 us
  starting transfers between devices: 34.4 us -> 7.52 us
    all_to_all x6 -> x1, waiting for transfers between devices: 216 us -> 0.01 us  [send_pages(): lax.all_to_all(sent.reshape(dev_count, capacity, width + HS), ('tp', 'sub...]
    dot_general x48 -> x2, matrix products: 176 us -> 2.45 us  [the longest x1 1.36 us: send_pages(): jnp.dot(pick, packed, preferred_element_type=jnp.float32)]
    pallas_call x0 -> x1, Pallas kernels: none -> 168 us  [fused(): pl.pallas_call(attend_kernel, out_shape=jax.ShapeDtypeStruct(queries.shap...]
    reduce_sum x25 -> x1, other arithmetic: 88.9 us -> 0.9 us  [send_pages(): within = jnp.sum(same_owner.astype(jnp.int32), axis=1)]
    reshape x8 -> x2, local copies, waits for them, and re-layouts: 29.8 us -> 1.52 us  [the longest x1 1.24 us: send_pages(): sent.reshape(dev_count, capacity, width + HS)]
    all_to_all x6 -> x1, starting transfers between devices: 34.4 us -> 7.52 us  [send_pages(): lax.all_to_all(sent.reshape(dev_count, capacity, width + HS), ('tp', 'sub...]
    unnamed x17 -> x3, local copies, waits for them, and re-layouts: 28.3 us -> 3.83 us
    all_to_all x6 -> x0, local copies, waits for them, and re-layouts: 22.8 us -> none  [the longest x1 10.7 us: shards(): lax.all_to_all(query_send, 'tp', split_axis=1, concat_axis=0, tiled=True)]
  transfers between devices with their start and end apart: 6 -> 1, of which waited for: 4 -> 0; matrix products, arithmetic and copies ran while one was open for 58% -> 1% of each run, Pallas kernels for 0% -> 89%
where the time goes in v1:
time: 189 us; the launch traced here: 188 us
  Pallas kernels  168 us (89%)
  starting transfers between devices  7.52 us (4%)
  local copies, waits for them, and re-layouts  6.1 us (3%)
  other arithmetic  3.65 us (2%)
  matrix products  2.45 us (1%)
    pallas_call x1, Pallas kernels, fused(): pl.pallas_call(attend_kernel, out_shape=jax.ShapeDtypeStruct(queries.shap...  168 us
    all_to_all x1, starting transfers between devices, send_pages(): lax.all_to_all(sent.reshape(dev_count, capacity, width + HS), ('tp', 'sub...  7.52 us
    unnamed x3, local copies, waits for them, and re-layouts  3.83 us
  transfers between devices with their start and end apart: 1, of which 0 were waited for; matrix products, arithmetic and copies ran while one was open for 1% of the time, Pallas kernels for 89%

profile of v1, /device:TPU:0, one launch (start us, length us, event | category | flops | bytes accessed | tf_op | source)
XLA Modules:
  0.0 188.2 jit_solution(6359651830778318181)
XLA Ops:
  0.6 0.7 add_convert_fusion
  1.3 0.9 convert_reduce_fusion
  2.2 0.7 multiply_add_fusion
  2.9 0.1 broadcast_in_dim.12
  2.9 1.4 convolution_convert_fusion
  4.3 1.2 reshape.35
  5.6 0.0 copy-start
  5.6 7.5 %all-to-all-start = ((bf16[16,9,2176]{2,1,0:T(8,128)(2,1)}), bf16[16,9,2176]{2,1,0:T(8,128)(2,1)S(1)}, u32[]{:S(2)}, u32[]{:S(2)}) async-start(bf16[16,9,2176]{2,1,0:T(8,128)(2,1)} %reshape.35), calls=%async_computation | async-start | bytes 2228224 | tf_op jit(solution)/shard_map/all_to_all | solution.py:370
  13.1 0.0 copy-done
  13.1 0.7 dynamic_slice.3
  13.8 1.3 compare_select_fusion.bias_ref
  15.1 167.8 %attend.1 = bf16[128,12288]{1,0:T(8,128)(2,1)} custom-call(bf16[128,12288]{1,0:T(8,128)(2,1)} %q_ref.1, bf16[128,2048]{1,0:T(8,128)(2,1)} %new_ref.1, bf16[2,512,2048]{2,1,0:T(8,128)(2,1)} %prefix_ref.1, f32[1,4096]{1,0:T(1,128)} %compare_select_fusion.bias_ref), custom_call_target="tpu_custom_call" | custom-call | flops 32212254720 | bytes 8388608 | tf_op jit(solution)/shard_map/attend/pallas_call | solution.py:386
  182.9 0.0 all-to-all-done
  182.9 0.3 reshape.36
  183.2 0.1 add_reduce_fusion
  183.3 1.1 convolution_convert_fusion.1
  184.4 3.8 %copy.9 = bf16[128,12288]{1,0:T(8,128)(2,1)} copy(bf16[128,12288]{1,0:T(8,128)(2,1)} %attend.1) | data formatting | bytes 6291456
Async XLA Ops:
  5.6 7.6 %copy-start = (s32[2]{0:T(128)S(1)}, s32[2]{0:T(128)}, u32[]{:S(2)}) copy-start(s32[2]{0:T(128)} %param.9) | copy-start | bytes 28
  5.6 177.4 %all-to-all-start = ((bf16[16,9,2176]{2,1,0:T(8,128)(2,1)}), bf16[16,9,2176]{2,1,0:T(8,128)(2,1)S(1)}, u32[]{:S(2)}, u32[]{:S(2)}) async-start(bf16[16,9,2176]{2,1,0:T(8,128)(2,1)} %reshape.35), calls=%async_computation | async-start | bytes 2228224 | tf_op jit(solution)/shard_map/all_to_all | solution.py:370

commit v2 on v1

--- a/solution.py
+++ b/solution.py
@@ -202,6 +202,9 @@
 
     def to_z(role, src):
         return copy(piece(src, s), piece(src, s), 20 + role, ici_sem.at[role], dev(zp, s))
+
+    def pass_z(role, src):
+        return copy(piece(src, s), piece(src, s), 27, ici_sem.at[role], dev(zp, s))
 
     def new_sib(role, tp):
         return copy(new_of(tp, s), new_of(tp, s), 24 + role, newsib_sem.at[role], dev(t, sp))
@@ -294,13 +297,24 @@
     earlier = lax.broadcasted_iota(jnp.int32, (1, count * rows), 1) < me * rows
     new_bias = jnp.where(earlier, 0.0, -1e30)
 
-    def arrive_first():
+    def first_inner():
+        across(0, zp)
+        across(3, yp)
+
+    def first_outer():
         column(0, zp)
-        across(3, yp)
+        got(3, yp)
+        pass_z(4, yp).start()
+        to_sib(3, yp).start()
+
+    def last_inner():
+        got(6, far_y)
+        pass_z(6, far_y).start()
+        to_sib(6, far_y).start()
 
     attend(
         [lambda cols, i=i: news[i, :, cols] for i in range(count)], lambda: new_bias, False,
-        [(7, None, arrive_first), (7, inner, lambda: column_inner(1, near))],
+        [(7, inner, first_inner), (7, outer, first_outer), (7, inner, lambda: column_inner(1, near))],
     )
     got_sib(0, zp)
     got_sib(3, yp)
@@ -317,15 +331,16 @@
     attend(
         [shard_cols(dp), shard_cols(near)], pair_bias(dp, near), False,
         [
-            (6, outer, lambda: column(2, far)),
+            (6, outer, lambda: across(2, far)),
             (7, None, lambda: across(5, near_y)),
+            (7, inner, last_inner),
         ],
     )
     got_sib(5, near_y)
     got_sib(2, far)
     attend(
         [shard_cols(near_y), shard_cols(far)], pair_bias(near_y, far), False,
-        [(6, None, lambda: across(6, far_y))],
+        [(6, outer, lambda: across(6, far_y))],
     )
     got_sib(6, far_y)
     attend([shard_cols(far_y)], lambda: shard_bias(far_y), False)
@@ -343,8 +358,7 @@
     cross_near.wait_send()
     for role, src in enumerate((zp, near, far, yp, dp, near_y, far_y)):
         to_sib(role, src).wait_send()
-    for role, src in enumerate((zp, near, far)):
-        to_y(role, src).wait_send()
+    to_y(1, near).wait_send()
     for role, tp in enumerate((zp, yp, dp)):
         new_sib(role, tp).wait_send()
 
@@ -352,6 +366,13 @@
     def _():
         to_z(1, near).wait_send()
         to_z(2, far).wait_send()
+        to_y(2, far).wait_send()
+        pass_z(6, far_y).wait_send()
+
+    @pl.when(outer)
+    def _():
+        to_y(0, zp).wait_send()
+        pass_z(4, yp).wait_send()
 
 
 def send_pages(new_kv, owner, slot):

time: 189 us -> 206 us (1.090)
  Pallas kernels: 168 us -> 185 us
    pallas_call x1, Pallas kernels: 168 us -> 185 us  [fused(): pl.pallas_call(attend_kernel, out_shape=jax.ShapeDtypeStruct(queries.shap...]
  transfers between devices with their start and end apart: 1 -> 1, of which waited for: 0 -> 0; matrix products, arithmetic and copies ran while one was open for 1% -> 1% of each run, Pallas kernels for 89% -> 90%
where the time goes in v2:
time: 206 us
  Pallas kernels  185 us (90%)
  starting transfers between devices  7.52 us (4%)
  local copies, waits for them, and re-layouts  6.1 us (3%)
  other arithmetic  3.65 us (2%)
  matrix products  2.45 us (1%)
    pallas_call x1, Pallas kernels, fused(): pl.pallas_call(attend_kernel, out_shape=jax.ShapeDtypeStruct(queries.shap...  185 us
    all_to_all x1, starting transfers between devices, send_pages(): lax.all_to_all(sent.reshape(dev_count, capacity, width + HS), ('tp', 'sub...  7.52 us
  transfers between devices with their start and end apart: 1, of which 0 were waited for; matrix products, arithmetic and copies ran while one was open for 1% of the time, Pallas kernels for 90%

profile of v2, /device:TPU:0, one launch (start us, length us, event | category | flops | bytes accessed | tf_op | source)
XLA Modules:
  0.0 205.5 jit_solution(6431517508521912189)
XLA Ops:
  0.6 0.7 add_convert_fusion
  1.3 0.9 convert_reduce_fusion
  2.2 0.7 multiply_add_fusion
  2.9 0.1 broadcast_in_dim.12
  2.9 1.4 convolution_convert_fusion
  4.3 1.2 reshape.35
  5.6 0.0 copy-start
  5.6 7.5 %all-to-all-start = ((bf16[16,9,2176]{2,1,0:T(8,128)(2,1)}), bf16[16,9,2176]{2,1,0:T(8,128)(2,1)S(1)}, u32[]{:S(2)}, u32[]{:S(2)}) async-start(bf16[16,9,2176]{2,1,0:T(8,128)(2,1)} %reshape.35), calls=%async_computation | async-start | bytes 2228224 | tf_op jit(solution)/shard_map/all_to_all | solution.py:391
  13.1 0.0 copy-done
  13.1 0.7 dynamic_slice.3
  13.8 1.3 compare_select_fusion.bias_ref
  15.1 185.1 %attend.1 = bf16[128,12288]{1,0:T(8,128)(2,1)} custom-call(bf16[128,12288]{1,0:T(8,128)(2,1)} %q_ref.1, bf16[128,2048]{1,0:T(8,128)(2,1)} %new_ref.1, bf16[2,512,2048]{2,1,0:T(8,128)(2,1)} %prefix_ref.1, f32[1,4096]{1,0:T(1,128)} %compare_select_fusion.bias_ref), custom_call_target="tpu_custom_call" | custom-call | flops 32212254720 | bytes 8388608 | tf_op jit(solution)/shard_map/attend/pallas_call | solution.py:407
  200.2 0.0 all-to-all-done
  200.2 0.3 reshape.36
  200.5 0.1 add_reduce_fusion
  200.6 1.1 convolution_convert_fusion.1
  201.7 3.8 %copy.9 = bf16[128,12288]{1,0:T(8,128)(2,1)} copy(bf16[128,12288]{1,0:T(8,128)(2,1)} %attend.1) | data formatting | bytes 6291456
Async XLA Ops:
  5.6 7.6 %copy-start = (s32[2]{0:T(128)S(1)}, s32[2]{0:T(128)}, u32[]{:S(2)}) copy-start(s32[2]{0:T(128)} %param.9) | copy-start | bytes 28
  5.6 194.6 %all-to-all-start = ((bf16[16,9,2176]{2,1,0:T(8,128)(2,1)}), bf16[16,9,2176]{2,1,0:T(8,128)(2,1)S(1)}, u32[]{:S(2)}, u32[]{:S(2)}) async-start(bf16[16,9,2176]{2,1,0:T(8,128)(2,1)} %reshape.35), calls=%async_computation | async-start | bytes 2228224 | tf_op jit(solution)/shard_map/all_to_all | solution.py:391
